TPU v7x, 32 devices: a whole 2x2x4 slice. The times are simulated.
32 devices in a mesh: groups: 2 (over x), node: 16 (over z, y, core), local: 1.
Axes of the slice: x: 2, y: 2, z: 4, core: 2. Of those that a mesh axis runs over, the one named last changes fastest.
Arguments:
- resid: bfloat16 [256, 3584], P(('groups', 'node', 'local')), parts along dimension 0, may hold values from -16 to 16
- prev_rows: bfloat16 [32, 1, 16, 4, 3584], P(('groups', 'node'), 'local'), parts along dimension 0, may hold values from -6 to 6
- prev_slots: int32 [256, 4], P(('groups', 'node', 'local')), parts along dimension 0, may hold values from 0 to 15, all different within a row; in each aligned block of 8 rows (0 to 7, 8 to 15, ...) at most 4 rows name the same one
- prev_gates: float32 [256, 4], P(('groups', 'node', 'local')), parts along dimension 0, may hold values from 0.1 to 0.9
- query: bfloat16 [256, 64, 576], P(('groups', 'node', 'local')), parts along dimension 0, may hold values from -8 to 8
- cache: bfloat16 [256, 192, 576], P(('groups', 'node', 'local')), parts along dimension 0, may hold values from -4 to 4
- lengths: int32 [256], P(('groups', 'node', 'local')), parts along dimension 0, may hold values from 24 to 192, as said below
- norm_gain: float32 [3584], replicated, may hold values from 0.1 to 1.9
- router: bfloat16 [3584, 14], replicated, may hold values from -0.09375 to 0.09375
- slot_expert: int32 [16], replicated, may hold values from 0 to 13, as said below
- expert_ids: int32 [256, 4], P(('groups', 'node', 'local')), parts along dimension 0, may hold values from 0 to 13, all different within a row; in each aligned block of 8 rows (0 to 7, 8 to 15, ...) at most 4 rows name the same one
- gate_up: bfloat16 [16, 3584, 2, 1024], P('node', None, None, 'local')
- down: bfloat16 [16, 1024, 3584], P('node', 'local')
Outputs:
- attended: bfloat16 [256, 64, 512], P(('groups', 'node', 'local')), parts along dimension 0
- mixed_out: bfloat16 [256, 3584], P(('groups', 'node', 'local')), parts along dimension 0
There are 2 independent parts, one for each index of `groups`. A program takes and returns all parts, laid end to end along the dimension named above; an argument that names none is the same for every part. Nothing has to cross between parts.
Inputs may be any that keep to these rules, and one draw needn't show every extreme that they name: `slot_expert`: each of the 14 experts sits in one slot or two; 2 of them sit in two. `prev_slots`: each row names 4 different slots; at most 4 rows of one device name one slot, and that many do in some device. `expert_ids`: each row names 4 different experts; at most 4 rows of one device name one expert, and that many do in some device. `lengths`: every device holds a request whose length is 192.
All inputs are finite; a program needn't handle non-finite values.
Results may differ from a plain program's by a relative error of at most 0.005.
Values may be sent and summed in bfloat16 or wider, within the bound.
A program may use at most 128 MiB of HBM per device.

v0:
```python
import jax
import jax.numpy as jnp
from jax import lax
from jax.sharding import PartitionSpec as P

LATENT = 512
ROPE = 64
NOPE = 128


def slot_places(targets):
    pair_count = targets.shape[0]
    same_slot = (targets[:, None] == targets[None, :]).astype(jnp.int32)
    earlier = (jnp.arange(pair_count)[None, :] < jnp.arange(pair_count)[:, None]).astype(jnp.int32)
    return jnp.sum(same_slot * earlier, axis=1)


def selector(targets, places, slot_count, capacity):
    column = jnp.arange(slot_count * capacity, dtype=jnp.int32)[None, :]
    return (column == (targets * capacity + places)[:, None]).astype(jnp.bfloat16)


def expert_partial(gathered, gate_up, down):
    features = gathered.shape[-1]
    unit_count = down.shape[1]
    flat_rows = gathered.reshape(-1, features)
    projected = jnp.dot(
        flat_rows, gate_up.reshape(features, 2 * unit_count), preferred_element_type=jnp.float32
    )
    hidden = (jax.nn.silu(projected[:, :unit_count]) * projected[:, unit_count:]).astype(
        jnp.bfloat16
    )
    partial_value = jnp.dot(
        hidden, down.reshape(unit_count, features), preferred_element_type=jnp.float32
    )
    return partial_value.reshape(gathered.shape)


def shards(
    resid,
    prev_rows,
    prev_slots,
    prev_gates,
    query,
    cache,
    lengths,
    norm_gain,
    router,
    slot_expert,
    expert_ids,
    gate_up,
    down,
):
    slot_count = lax.axis_size("node")
    core_count = lax.axis_size("local")
    row_count, features = resid.shape
    top_k = expert_ids.shape[1]
    pair_count = row_count * top_k
    capacity = prev_rows.shape[3]
    returned = lax.all_to_all(
        prev_rows.reshape(slot_count, capacity, features),
        "node",
        split_axis=0,
        concat_axis=0,
        tiled=True,
    )
    prev_targets = prev_slots.reshape(pair_count)
    prev_pick = selector(prev_targets, slot_places(prev_targets), slot_count, capacity)
    values = jnp.dot(
        prev_pick,
        returned.reshape(slot_count * capacity, features),
        preferred_element_type=jnp.float32,
    )
    values = values.reshape(row_count, top_k, features)
    residual = resid.astype(jnp.float32) + jnp.sum(prev_gates[:, :, None] * values, axis=1)
    mean_square = jnp.mean(residual * residual, axis=1, keepdims=True)
    normed = (residual * lax.rsqrt(mean_square + 1e-06) * norm_gain[None, :]).astype(jnp.bfloat16)
    logits = jnp.dot(normed, router, preferred_element_type=jnp.float32)
    expert_count = router.shape[1]
    chosen = expert_ids[:, :, None] == jnp.arange(expert_count, dtype=jnp.int32)[None, None, :]
    picked = jnp.sum(jnp.where(chosen, logits[:, None, :], 0.0), axis=2)
    score = jax.nn.sigmoid(picked)
    gate_weight = 2.5 * score / jnp.sum(score, axis=1, keepdims=True)
    flat_ids = expert_ids.reshape(pair_count)
    holds_it = slot_expert[None, :] == flat_ids[:, None]
    slot_index = jnp.arange(slot_count, dtype=jnp.int32)[None, :]
    targets = jnp.min(jnp.where(holds_it, slot_index, slot_count), axis=1)
    pick = selector(targets, slot_places(targets), slot_count, capacity)
    repeated = jnp.broadcast_to(normed[:, None, :], (row_count, top_k, features)).reshape(
        pair_count, features
    )
    outgoing = jnp.einsum("pk,pd->kd", pick, repeated, preferred_element_type=jnp.float32).astype(
        jnp.bfloat16
    )
    outgoing = outgoing.reshape(slot_count, capacity, features)
    doubled = jnp.broadcast_to(outgoing[:, None], (slot_count, core_count, capacity, features))
    doubled = doubled.reshape(slot_count * core_count, capacity, features)
    arrived = lax.all_to_all(doubled, ("node", "local"), split_axis=0, concat_axis=0, tiled=True)
    gathered = arrived.reshape(slot_count, core_count, capacity, features)
    partial_value = expert_partial(gathered, gate_up, down)
    summed = lax.psum_scatter(partial_value, "local", scatter_dimension=1, tiled=True)
    expert_out = summed.astype(jnp.bfloat16).reshape(slot_count, capacity, features)
    came_back = lax.all_to_all(expert_out, "node", split_axis=0, concat_axis=0, tiled=True)
    outputs = jnp.dot(
        pick, came_back.reshape(slot_count * capacity, features), preferred_element_type=jnp.float32
    )
    outputs = outputs.reshape(row_count, top_k, features)
    routed = jnp.sum(gate_weight[:, :, None] * outputs, axis=1)
    mixed_out = (residual + routed).astype(jnp.bfloat16)
    score_scale = (NOPE + ROPE) ** (-0.5)
    scores = (
        jnp.einsum("thc,tlc->thl", query, cache, preferred_element_type=jnp.float32) * score_scale
    )
    positions = cache.shape[1]
    in_range = jnp.arange(positions)[None, None, :] < lengths[:, None, None]
    scores = jnp.where(in_range, scores, -1e30)
    row_max = jnp.max(scores, axis=2, keepdims=True)
    expo = jnp.where(in_range, jnp.exp(scores - row_max), 0.0)
    weights = (expo / jnp.sum(expo, axis=2, keepdims=True)).astype(jnp.bfloat16)
    attended = jnp.einsum(
        "thl,tlc->thc", weights, cache[:, :, :LATENT], preferred_element_type=jnp.float32
    )
    return (attended.astype(jnp.bfloat16), mixed_out)


def solution(mesh):
    return jax.shard_map(
        shards,
        mesh=mesh,
        in_specs=(
            P(("groups", "node", "local"), None),
            P(("groups", "node"), "local", None, None, None),
            P(("groups", "node", "local"), None),
            P(("groups", "node", "local"), None),
            P(("groups", "node", "local"), None, None),
            P(("groups", "node", "local"), None, None),
            P(("groups", "node", "local")),
            P(),
            P(),
            P(),
            P(("groups", "node", "local"), None),
            P("node", None, None, "local"),
            P("node", "local", None),
        ),
        out_specs=(
            P(("groups", "node", "local"), None, None),
            P(("groups", "node", "local"), None),
        ),
        check_vma=False,
    )
```

profile of v0, /device:TPU:0, one launch (start us, length us, event | category | flops | bytes accessed | tf_op | source)
XLA Modules:
  0.0 84.7 jit_solution(12356228492677787152)
XLA Ops:
  0.6 7.5 %all-to-all-start = ((bf16[16,4,3584]{2,1,0:T(4,128)(2,1)}), bf16[16,4,3584]{2,1,0:T(4,128)(2,1)S(1)}, u32[]{:S(2)}, u32[]{:S(2)}) async-start(bf16[16,4,3584]{2,1,0:T(4,128)(2,1)} %bitcast.29), calls=%async_computation | async-start | bytes 917504 | tf_op jit(solution)/shard_map/all_to_all | solution.py:60
  8.2 0.8 copy.38
  9.0 0.2 select_reduce_fusion.2
  9.4 0.8 copy.41
  10.2 0.7 select_reduce_fusion.3
  11.0 0.2 select_reduce_fusion
  11.2 10.3 %all-to-all-done = bf16[16,4,3584]{2,1,0:T(4,128)(2,1)S(1)} async-done(((bf16[16,4,3584]{2,1,0:T(4,128)(2,1)}), bf16[16,4,3584]{2,1,0:T(4,128)(2,1)S(1)}, u32[]{:S(2)}, u32[]{:S(2)}) %all-to-all-start) | async-done | bytes 458784 | tf_op jit(solution)/shard_map/all_to_all | solution.py:60
  21.4 0.1 reshape.167
  21.5 1.0 %fusion.15 = f32[8,3584]{1,0:T(8,128)S(1)} fusion(bf16[64,3584,1]{1,0,2:T(8,128)(2,1)S(1)} %reshape.167, f32[8,4]{0,1:T(4,128)} %param.16, s32[8,4]{0,1:T(4,128)S(1)} %copy.40), kind=kOutput, calls=%fused_computation.15 | convolution fusion | flops 14882816 | bytes 573696 | tf_op jit(solution)/shard_map/dot_general | solution.py:69
  22.5 1.0 %multiply_reduce_fusion = f32[8]{0:T(128)S(1)} fusion(f32[8,3584]{1,0:T(8,128)S(1)} %fusion.15, bf16[8,3584]{1,0:T(8,128)(2,1)} %param.13), kind=kLoop, calls=%fused_computation.24 | loop fusion | flops 114680 | bytes 172064 | tf_op jit(solution)/shard_map/reduce_sum | solution.py:76
  23.5 0.9 %multiply_convert_fusion = bf16[8,3584]{1,0:T(8,128)(2,1)S(1)} fusion(f32[3584]{0:T(1024)} %param.20, f32[8]{0:T(128)S(1)} %add_rsqrt_fusion, f32[8,3584]{1,0:T(8,128)S(1)} %fusion.15, bf16[8,3584]{1,0:T(8,128)(2,1)} %param.13), kind=kLoop, calls=%fused_computation.23 | loop fusion | flops 143360 | bytes 243744 | tf_op jit(solution)/shard_map/convert_element_type | solution.py:77
  24.5 0.6 copy-done.5
  25.2 0.4 convolution_convert_fusion
  25.6 0.9 %reshape_broadcast_in_dim_reshape.3 = bf16[16,4,3584]{2,1,0:T(4,128)(2,1)} reshape(bf16[64,3584]{1,0:T(8,128)(2,1)S(1)} %convolution_convert_fusion) | data formatting | bytes 917504 | tf_op jit(solution)/shard_map/reshape;broadcast_in_dim;reshape | solution.py:97
  26.5 3.9 %all-to-all-start.1 = ((bf16[16,4,3584]{2,1,0:T(4,128)(2,1)}), bf16[16,4,3584]{2,1,0:T(4,128)(2,1)S(1)}, u32[]{:S(2)}, u32[]{:S(2)}) async-start(bf16[16,4,3584]{2,1,0:T(4,128)(2,1)} %reshape_broadcast_in_dim_reshape.3), calls=%async_computation.1 | async-start | bytes 917504 | tf_op jit(solution)/shard_map/all_to_all | solution.py:98
  30.5 16.2 %copy.45 = bf16[448,8,2,1024]{3,1,2,0:T(8,128)(2,1)} copy(bf16[448,8,2,1024]{3,2,1,0:T(2,128)(2,1)} %bitcast.28) | data formatting | bytes 29360128
  46.7 0.6 copy.42
  47.4 0.9 %fusion.14 = f32[8,64,192]{2,1,0:T(8,128)S(1)} fusion(bf16[8,64,576]{2,1,0:T(8,128)(2,1)S(1)} %copy-done, bf16[8,192,576]{2,1,0:T(8,128)(2,1)S(1)} %copy-done.1, pred[8,192]{1,0:T(8,128)(4,1)S(1)} %iota_compare_fusion.6), kind=kOutput, calls=%fused_computation.14 | convolution fusion | flops 113442816 | bytes 2754048 | tf_op jit(solution)/shard_map/thc,tlc->thl/dot_general | solution.py:112
  48.3 0.8 copy-done.4
  49.1 0.8 fusion.30
  50.0 0.1 reshape_reshape.3
  50.1 7.8 %fusion.32 = f32[64,2048]{1,0:T(8,128)S(1)} fusion(bf16[64,3584]{1,0:T(8,128)(2,1)S(1)} %reshape_reshape.3, bf16[3584,2048]{1,0:T(8,128)(2,1)} %bitcast.27), kind=kOutput, calls=%fused_computation.51 | convolution fusion | flops 939524096 | bytes 15663104 | tf_op jit(solution)/shard_map/dot_general | solution.py:27
  58.1 4.5 %fusion.3 = bf16[16,4,3584]{2,0,1:T(8,128)(2,1)S(1)} fusion(bf16[1,1024,3584]{2,1,0:T(8,128)(2,1)} %param.25, bf16[16,4,1024]{2,1,0:T(4,128)(2,1)S(1)} %dot_general.32), kind=kOutput, calls=%fused_computation.3 | convolution fusion | flops 469991424 | bytes 7929856 | tf_op jit(solution)/shard_map/dot_general | solution.py:33
  62.6 1.1 %copy.44 = bf16[16,4,3584]{2,1,0:T(4,128)(2,1)} copy(bf16[16,4,3584]{2,0,1:T(8,128)(2,1)S(1)} %fusion.3) | data formatting | bytes 917504 | tf_op jit(solution)/shard_map/convert_element_type | solution.py:102
  63.8 6.0 %all-to-all-start.2 = ((bf16[16,4,3584]{2,1,0:T(4,128)(2,1)}), bf16[16,4,3584]{2,1,0:T(4,128)(2,1)S(1)}, u32[]{:S(2)}, u32[]{:S(2)}) async-start(bf16[16,4,3584]{2,1,0:T(4,128)(2,1)} %copy.44), calls=%async_computation.2 | async-start | bytes 917504 | tf_op jit(solution)/shard_map/all_to_all | solution.py:103
  69.8 3.0 %fusion.8 = bf16[8,64,512]{2,1,0:T(8,128)(2,1)} fusion(bf16[8,192,576]{2,1,0:T(8,128)(2,1)S(1)} %copy-done.1, f32[8,64]{1,0:T(8,128)} %fusion.30, f32[8,64,192]{2,1,0:T(8,128)} %copy-done.4, pred[8,192]{1,0:T(8,128)(4,1)} %copy-done.9), kind=kOutput, calls=%fused_computation.9 | convolution fusion | flops 101319360 | bytes 3151872 | tf_op jit(solution)/shard_map/thl,tlc->thc/dot_general | solution.py:120
  72.8 0.1 fusion.31
  72.9 0.9 %select_reduce_fusion.1 = f32[8,4]{0,1:T(4,128)S(1)} fusion(f32[8,14]{1,0:T(8,128)S(1)} %fusion.31, s32[8,4]{0,1:T(4,128)} %param.23), kind=kLoop, calls=%fused_computation.29 | loop fusion | flops 1312 | bytes 704 | tf_op jit(solution)/shard_map/reduce_sum | solution.py:81
  73.8 9.2 %all-to-all-done.2 = bf16[16,4,3584]{2,1,0:T(4,128)(2,1)S(1)} async-done(((bf16[16,4,3584]{2,1,0:T(4,128)(2,1)}), bf16[16,4,3584]{2,1,0:T(4,128)(2,1)S(1)}, u32[]{:S(2)}, u32[]{:S(2)}) %all-to-all-start.2) | async-done | bytes 458784 | tf_op jit(solution)/shard_map/all_to_all | solution.py:103
  83.0 0.1 reshape.169
  83.1 0.9 %fusion.16 = f32[8,3584]{1,0:T(8,128)S(1)} fusion(bf16[64,3584,1]{1,0,2:T(8,128)(2,1)S(1)} %reshape.169, f32[8,4]{0,1:T(4,128)S(1)} %multiply_divide_fusion, s32[8,4]{0,1:T(4,128)} %copy.42), kind=kOutput, calls=%fused_computation.16 | convolution fusion | flops 14882816 | bytes 573696 | tf_op jit(solution)/shard_map/dot_general | solution.py:104
  84.1 0.6 add_convert_fusion
  (36 shorter events, 0.9 us)
Async XLA Ops:
  0.6 46.8 %copy-start = (bf16[8,64,576]{2,1,0:T(8,128)(2,1)S(1)}, bf16[8,64,576]{2,1,0:T(8,128)(2,1)}, u32[]{:S(2)}) copy-start(bf16[8,64,576]{2,1,0:T(8,128)(2,1)} %param.17) | copy-start | bytes 1769476
  0.6 20.8 %all-to-all-start = ((bf16[16,4,3584]{2,1,0:T(4,128)(2,1)}), bf16[16,4,3584]{2,1,0:T(4,128)(2,1)S(1)}, u32[]{:S(2)}, u32[]{:S(2)}) async-start(bf16[16,4,3584]{2,1,0:T(4,128)(2,1)} %bitcast.29), calls=%async_computation | async-start | bytes 917504 | tf_op jit(solution)/shard_map/all_to_all | solution.py:60
  22.5 1.0 %copy-start.2 = (f32[8,3584]{1,0:T(8,128)}, f32[8,3584]{1,0:T(8,128)S(1)}, u32[]{:S(2)}) copy-start(f32[8,3584]{1,0:T(8,128)S(1)} %fusion.15) | copy-start | bytes 344068
  24.5 0.6 copy-start.5
  26.5 23.5 %all-to-all-start.1 = ((bf16[16,4,3584]{2,1,0:T(4,128)(2,1)}), bf16[16,4,3584]{2,1,0:T(4,128)(2,1)S(1)}, u32[]{:S(2)}, u32[]{:S(2)}) async-start(bf16[16,4,3584]{2,1,0:T(4,128)(2,1)} %reshape_broadcast_in_dim_reshape.3), calls=%async_computation.1 | async-start | bytes 917504 | tf_op jit(solution)/shard_map/all_to_all | solution.py:98
  30.5 16.8 %copy-start.10 = (s32[8]{0:T(128)S(1)}, s32[8]{0:T(128)}, u32[]{:S(2)}) copy-start(s32[8]{0:T(128)} %param.19) | copy-start | bytes 100
  30.5 16.9 %copy-start.1 = (bf16[8,192,576]{2,1,0:T(8,128)(2,1)S(1)}, bf16[8,192,576]{2,1,0:T(8,128)(2,1)}, u32[]{:S(2)}) copy-start(bf16[8,192,576]{2,1,0:T(8,128)(2,1)} %param.18) | copy-start | bytes 5308420
  47.4 0.9 %copy-start.9 = (pred[8,192]{1,0:T(8,128)(4,1)}, pred[8,192]{1,0:T(8,128)(4,1)S(1)}, u32[]{:S(2)}) copy-start(pred[8,192]{1,0:T(8,128)(4,1)S(1)} %iota_compare_fusion.6) | copy-start | bytes 4612
  48.3 0.8 copy-start.4
  58.0 14.8 %copy-start.6 = (bf16[8,3584]{1,0:T(8,128)(2,1)S(1)}, bf16[8,3584]{1,0:T(8,128)(2,1)}, u32[]{:S(2)}) copy-start(bf16[8,3584]{1,0:T(8,128)(2,1)} %copy-done.5) | copy-start | bytes 172036
  58.1 14.7 %copy-start.8 = (bf16[3584,14]{0,1:T(8,128)(2,1)S(1)}, bf16[3584,14]{0,1:T(8,128)(2,1)}, u32[]{:S(2)}) copy-start(bf16[3584,14]{0,1:T(8,128)(2,1)} %param.21) | copy-start | bytes 301060
  58.1 26.0 %copy-start.3 = (f32[8,3584]{1,0:T(8,128)S(1)}, f32[8,3584]{1,0:T(8,128)}, u32[]{:S(2)}) copy-start(f32[8,3584]{1,0:T(8,128)} %copy-done.2) | copy-start | bytes 344068
  58.1 26.0 %copy-start.7 = (bf16[8,3584]{1,0:T(8,128)(2,1)S(1)}, bf16[8,3584]{1,0:T(8,128)(2,1)}, u32[]{:S(2)}) copy-start(bf16[8,3584]{1,0:T(8,128)(2,1)} %param.13) | copy-start | bytes 172036
  63.8 19.3 %all-to-all-start.2 = ((bf16[16,4,3584]{2,1,0:T(4,128)(2,1)}), bf16[16,4,3584]{2,1,0:T(4,128)(2,1)S(1)}, u32[]{:S(2)}, u32[]{:S(2)}) async-start(bf16[16,4,3584]{2,1,0:T(4,128)(2,1)} %copy.44), calls=%async_computation.2 | async-start | bytes 917504 | tf_op jit(solution)/shard_map/all_to_all | solution.py:103
where the time goes:
time: 85.5 us; the launch traced here: 84.7 us
  local copies, waits for them, and re-layouts  22.8 us (27%)
  waiting for transfers between devices  19.5 us (23%)
  matrix products  18.6 us (22%)
  starting transfers between devices  17.4 us (20%)
  other arithmetic  5.59 us (7%)
    unnamed x25, local copies, waits for them, and re-layouts  19.2 us
    all_to_all x1, waiting for transfers between devices, shards(): lax.all_to_all(prev_rows.reshape(slot_count, capacity, features), 'node',...  10.3 us
    all_to_all x1, waiting for transfers between devices, shards(): lax.all_to_all(expert_out, 'node', split_axis=0, concat_axis=0, tiled=True)  9.19 us
    dot_general x1, matrix products, expert_partial(): jnp.dot(flat_rows, gate_up.reshape(features, 2 * unit_count), preferred_e...  7.82 us
    all_to_all x1, starting transfers between devices, shards(): lax.all_to_all(prev_rows.reshape(slot_count, capacity, features), 'node',...  7.53 us
    all_to_all x1, starting transfers between devices, shards(): lax.all_to_all(expert_out, 'node', split_axis=0, concat_axis=0, tiled=True)  6.01 us
    dot_general x1, matrix products, expert_partial(): jnp.dot(hidden, down.reshape(unit_count, features), preferred_element_typ...  4.53 us
    all_to_all x1, starting transfers between devices, shards(): lax.all_to_all(doubled, ('node', 'local'), split_axis=0, concat_axis=0, t...  3.89 us
  transfers between devices with their start and end apart: 3, of which 2 were waited for; matrix products, arithmetic and copies ran while one was open for 30% of the time, Pallas kernels for 0%

commit v1 on v0

--- a/solution.py
+++ b/solution.py
@@ -1,6 +1,10 @@
+import functools
+
 import jax
 import jax.numpy as jnp
 from jax import lax
+from jax.experimental import pallas as pl
+from jax.experimental.pallas import tpu as pltpu
 from jax.sharding import PartitionSpec as P
 
 LATENT = 512
@@ -123,9 +127,445 @@
     return (attended.astype(jnp.bfloat16), mixed_out)
 
 
+LANES = 128
+MESH = pl.DeviceIdType.MESH
+F32 = jnp.float32
+BF16 = jnp.bfloat16
+
+
+def remote(src, dst, send_sem, recv_sem, peer):
+    return pltpu.make_async_remote_copy(
+        src_ref=src,
+        dst_ref=dst,
+        send_sem=send_sem,
+        recv_sem=recv_sem,
+        device_id={"node": peer},
+        device_id_type=MESH,
+    )
+
+
+def columns_of(ref):
+    top_k, rows = ref.shape
+    values = ref[...].astype(F32)
+    diagonal = lax.broadcasted_iota(jnp.int32, (rows, rows), 0) == lax.broadcasted_iota(
+        jnp.int32, (rows, rows), 1
+    )
+    return [
+        jnp.sum(
+            jnp.where(diagonal, jnp.broadcast_to(values[k : k + 1, :], (rows, rows)), 0.0),
+            axis=1,
+            keepdims=True,
+        )
+        for k in range(top_k)
+    ]
+
+
+def fused_kernel(
+    n,
+    lengths_ref,
+    slot_expert_ref,
+    resid_ref,
+    slots_ref,
+    gates_ref,
+    gain_ref,
+    router_ref,
+    ids_ref,
+    prev_hbm,
+    query_hbm,
+    cache_hbm,
+    gate_up_hbm,
+    down_hbm,
+    attended_hbm,
+    mixed_ref,
+    prev_in,
+    prev_f32,
+    query_v,
+    cache_v,
+    attended_v,
+    wide_v,
+    down_v,
+    blocks,
+    spread,
+    hidden_v,
+    partial_v,
+    out_blocks,
+    core_in,
+    side_out,
+    side_in,
+    far_out,
+    far_in,
+    residual_v,
+    local_sem,
+    wide_sem,
+    prev_send,
+    prev_recv,
+    gather_send,
+    gather_recv,
+    sum_send,
+    sum_recv,
+):
+    me = lax.axis_index("node")
+    depth = n // 4
+    z, y, c = me // 4, (me // 2) % 2, me % 2
+    rows, features = resid_ref.shape
+    capacity = prev_hbm.shape[3]
+    units = down_v.shape[0]
+    strips = units // LANES
+
+    query_copy = pltpu.make_async_copy(query_hbm, query_v, local_sem.at[0])
+    cache_copy = pltpu.make_async_copy(cache_hbm, cache_v, local_sem.at[1])
+    down_copy = pltpu.make_async_copy(down_hbm.at[0], down_v, local_sem.at[2])
+    own_prev = pltpu.make_async_copy(prev_hbm.at[0, 0, me], prev_in.at[me], local_sem.at[3])
+
+    def strip_copy(i):
+        return pltpu.make_async_copy(
+            gate_up_hbm.at[0, :, :, pl.ds(i * LANES, LANES)], wide_v.at[i], wide_sem.at[i]
+        )
+
+    query_copy.start()
+    cache_copy.start()
+    own_prev.start()
+
+    barrier = pltpu.get_barrier_semaphore()
+
+    def greet(step, carry):
+        pl.semaphore_signal(
+            barrier, inc=1, device_id={"node": lax.rem(me + step, n)}, device_id_type=MESH
+        )
+        return carry
+
+    lax.fori_loop(1, n, greet, 0)
+    pl.semaphore_wait(barrier, n - 1)
+
+    def prev_copy(step):
+        peer = lax.rem(me + step, n)
+        return remote(
+            prev_hbm.at[0, 0, peer], prev_in.at[me], prev_send.at[step], prev_recv.at[me], peer
+        )
+
+    def send_prev(step, carry):
+        prev_copy(step).start()
+        return carry
+
+    lax.fori_loop(1, n, send_prev, 0)
+    for i in range(strips):
+        strip_copy(i).start()
+    down_copy.start()
+
+    query_copy.wait()
+    cache_copy.wait()
+    positions = cache_v.shape[1]
+    heads = query_v.shape[1]
+
+    def attend(r, carry):
+        keys = cache_v[r]
+        scores = lax.dot_general(
+            query_v[r], keys, (((1,), (1,)), ((), ())), preferred_element_type=F32
+        ) * ((NOPE + ROPE) ** (-0.5))
+        live = lax.broadcasted_iota(jnp.int32, (heads, positions), 1) < lengths_ref[r]
+        scores = jnp.where(live, scores, -1e30)
+        row_max = jnp.max(scores, axis=1, keepdims=True)
+        expo = jnp.where(live, jnp.exp(scores - row_max), 0.0)
+        weights = (expo / jnp.sum(expo, axis=1, keepdims=True)).astype(BF16)
+        attended_v[r] = jnp.dot(
+            weights, keys[:, :LATENT], preferred_element_type=F32
+        ).astype(BF16)
+        return carry
+
+    lax.fori_loop(0, query_v.shape[0], attend, 0)
+    attended_copy = pltpu.make_async_copy(attended_v, attended_hbm, local_sem.at[4])
+    attended_copy.start()
+
+    width = n * capacity
+    lane = lax.broadcasted_iota(jnp.int32, (rows, width), 1)
+    lane_slot = (lane // capacity).astype(F32)
+    lane_place = (lane % capacity).astype(F32)
+    uses = jnp.zeros((rows, width), F32)
+    gate_row = jnp.zeros((rows, width), F32)
+    for slot, gate in zip(columns_of(slots_ref), columns_of(gates_ref)):
+        hit = lane_slot == slot
+        uses = uses + jnp.where(hit, 1.0, 0.0)
+        gate_row = gate_row + jnp.where(hit, gate, 0.0)
+    token = lax.broadcasted_iota(jnp.int32, (rows, width), 0)
+    places = jnp.zeros((rows, width), F32)
+    for t in range(rows - 1):
+        places = places + jnp.where(token > t, uses[t : t + 1, :], 0.0)
+    gate_row = jnp.where(places == lane_place, gate_row, 0.0)
+    gate_high = gate_row.astype(BF16)
+    rest = gate_row - gate_high.astype(F32)
+    gate_mid = rest.astype(BF16)
+    gate_low = (rest - gate_mid.astype(F32)).astype(BF16)
+
+    slot_lane = lax.broadcasted_iota(jnp.int32, (1, LANES), 1)
+    held = jnp.full((1, LANES), -1, jnp.int32)
+    for i in range(n):
+        held = jnp.where(slot_lane == i, slot_expert_ref[i], held)
+    first = jnp.ones((1, LANES), F32)
+    for i in range(n):
+        first = jnp.where((held == slot_expert_ref[i]) & (slot_lane > i), 0.0, first)
+    held = held.astype(F32)
+
+    own_prev.wait()
+
+    def take_prev(step, carry):
+        source = lax.rem(me + step, n)
+        remote(
+            prev_hbm.at[0, 0, me], prev_in.at[source], prev_send.at[step], prev_recv.at[source],
+            source,
+        ).wait_recv()
+        return carry
+
+    lax.fori_loop(1, n, take_prev, 0)
+    for i in range(n):
+        prev_f32[i * capacity : (i + 1) * capacity, :] = prev_in[i].astype(F32)
+    prev_rows = prev_f32[...].astype(BF16)
+    combined = (
+        jnp.dot(gate_high, prev_rows, preferred_element_type=F32)
+        + jnp.dot(gate_mid, prev_rows, preferred_element_type=F32)
+        + jnp.dot(gate_low, prev_rows, preferred_element_type=F32)
+    )
+    residual = resid_ref[...].astype(F32) + combined
+    residual_v[...] = residual
+    mean_square = jnp.sum(residual * residual, axis=1, keepdims=True) * (1.0 / features)
+    normed = (residual * lax.rsqrt(mean_square + 1e-06) * gain_ref[...]).astype(BF16)
+    logits = lax.dot_general(
+        normed, router_ref[...], (((1,), (1,)), ((), ())), preferred_element_type=F32
+    )
+    expert_lane = lax.broadcasted_iota(jnp.int32, logits.shape, 1).astype(F32)
+    ids = columns_of(ids_ref)
+    picked = [
+        jnp.sum(jnp.where(expert_lane == chosen, logits, 0.0), axis=1, keepdims=True)
+        for chosen in ids
+    ]
+    score = [1.0 / (1.0 + jnp.exp(-value)) for value in picked]
+    total = functools.reduce(lambda a, b: a + b, score)
+    slot_weight = jnp.zeros((rows, LANES), F32)
+    for chosen, value in zip(ids, score):
+        slot_weight = slot_weight + jnp.where(held == chosen, 2.5 * value / total, 0.0)
+    slot_weight = slot_weight * first
+    weight_high = slot_weight.astype(BF16)
+    weight_low = (slot_weight - weight_high.astype(F32)).astype(BF16)
+    blocks[me, :, :features] = normed
+    blocks[me, :, features : features + LANES] = weight_high
+    blocks[me, :, features + LANES :] = weight_low
+
+    across, sibling = z * 4 + (1 - y) * 2 + c, z * 4 + y * 2 + (1 - c)
+    started = []
+
+    def send_block(index, peer):
+        copy = remote(
+            blocks.at[index], blocks.at[index], gather_send.at[len(started)],
+            gather_recv.at[index], peer,
+        )
+        copy.start()
+        started.append(copy)
+
+    def await_block(index):
+        remote(
+            blocks.at[index], blocks.at[index], gather_send.at[0], gather_recv.at[index], sibling
+        ).wait_recv()
+
+    for d in range(1, depth):
+        send_block(me, lax.rem(z + d, depth) * 4 + y * 2 + c)
+    send_block(me, across)
+    send_block(me, sibling)
+    await_block(across)
+    send_block(across, sibling)
+    for d in range(1, depth):
+        other = lax.rem(z + d, depth) * 4 + y * 2 + c
+        await_block(other)
+        send_block(other, across)
+        send_block(other, sibling)
+    for d in range(1, depth):
+        other = lax.rem(z + d, depth) * 4 + (1 - y) * 2 + c
+        await_block(other)
+        send_block(other, sibling)
+    for d in range(depth):
+        for side in range(2):
+            await_block(lax.rem(z + d, depth) * 4 + side * 2 + (1 - c))
+    for i in range(strips):
+        strip_copy(i).wait()
+
+    tokens = n * rows
+    low = lax.broadcasted_iota(jnp.int32, (LANES, 4 * LANES), 0)
+    high = lax.broadcasted_iota(jnp.int32, (LANES, 4 * LANES), 1)
+    dealt = jnp.where(
+        (high == 2 * low) | (high == 2 * low + 1 + 2 * LANES), 1.0, 0.0
+    ).astype(BF16)
+    for b in range(features // LANES):
+        part = blocks[:, :, b * LANES : (b + 1) * LANES].astype(F32).reshape(tokens, LANES)
+        both = jnp.dot(part.astype(BF16), dealt, preferred_element_type=F32).astype(BF16)
+        spread[:tokens, b * 2 * LANES : (b + 1) * 2 * LANES] = both[:, : 2 * LANES]
+        spread[tokens:, b * 2 * LANES : (b + 1) * 2 * LANES] = both[:, 2 * LANES :]
+    tail = blocks[:, :, features:].astype(F32).reshape(tokens, 2 * LANES)
+    tail_lane = lax.broadcasted_iota(jnp.int32, tail.shape, 1)
+    mine = jnp.sum(
+        jnp.where((tail_lane == me) | (tail_lane == me + LANES), tail, 0.0), axis=1, keepdims=True
+    )
+
+    def project(p, carry):
+        weights = jnp.concatenate(
+            [
+                wide_v.at[2 * p].reshape(2 * features, LANES)[...],
+                wide_v.at[2 * p + 1].reshape(2 * features, LANES)[...],
+            ],
+            axis=1,
+        )
+        projected = jnp.dot(spread[...], weights, preferred_element_type=F32)
+        gate, up = projected[:tokens], projected[tokens:]
+        hidden_v[p] = (gate / (1.0 + jnp.exp(-gate)) * up).astype(BF16)
+        return carry
+
+    lax.fori_loop(0, strips // 2, project, 0)
+    down_copy.wait()
+    hidden = jnp.concatenate([hidden_v[p] for p in range(strips // 2)], axis=1)
+    step = 512
+    for b in range(features // step):
+        span = slice(b * step, (b + 1) * step)
+        value = jnp.dot(hidden, down_v[:, span], preferred_element_type=F32) * mine
+        value = value.reshape(n, rows, step)
+        partial_v[:, :, span] = value
+        out_blocks[:, :, span] = value.astype(BF16)
+
+    sums = []
+
+    def send_sum(src, dst, send_index, recv_index, peer):
+        copy = remote(src, dst, sum_send.at[send_index], sum_recv.at[recv_index], peer)
+        copy.start()
+        sums.append(copy)
+
+    def await_sum(dst, index):
+        remote(dst, dst, sum_send.at[0], sum_recv.at[index], sibling).wait_recv()
+
+    order = list(range(1, depth)) + [0]
+    lines = [lax.rem(z + d, depth) for d in order]
+    for line in lines:
+        for side in (1 - y, y):
+            send_sum(
+                out_blocks.at[line * 4 + side * 2 + (1 - c)], core_in.at[line * 2 + side],
+                len(sums), line * 2 + side, sibling,
+            )
+    for line in lines:
+        await_sum(core_in.at[line * 2 + (1 - y)], line * 2 + (1 - y))
+        value = partial_v[line * 4 + (1 - y) * 2 + c] + core_in[line * 2 + (1 - y)].astype(F32)
+        side_out[line] = value.astype(BF16)
+        send_sum(side_out.at[line], side_in.at[line], len(sums), 2 * depth + line, across)
+        await_sum(core_in.at[line * 2 + y], line * 2 + y)
+        partial_v[line * 4 + y * 2 + c] += core_in[line * 2 + y].astype(F32)
+    for line in lines:
+        await_sum(side_in.at[line], 2 * depth + line)
+        value = partial_v[line * 4 + y * 2 + c] + side_in[line].astype(F32)
+        if line is lines[-1]:
+            residual_v[...] += value
+        else:
+            far_out[line] = value.astype(BF16)
+            send_sum(
+                far_out.at[line], far_in.at[z], len(sums), 3 * depth + z, line * 4 + y * 2 + c
+            )
+    for line in lines[:-1]:
+        await_sum(far_in.at[line], 3 * depth + line)
+        residual_v[...] += far_in[line].astype(F32)
+    mixed_ref[...] = residual_v[...].astype(BF16)
+
+    def sent_prev(step, carry):
+        prev_copy(step).wait_send()
+        return carry
+
+    lax.fori_loop(1, n, sent_prev, 0)
+    for copy in started + sums:
+        copy.wait_send()
+    attended_copy.wait()
+
+
+def fused_shards(
+    resid,
+    prev_rows,
+    prev_slots,
+    prev_gates,
+    query,
+    cache,
+    lengths,
+    norm_gain,
+    router,
+    slot_expert,
+    expert_ids,
+    gate_up,
+    down,
+):
+    n = lax.axis_size("node")
+    rows, features = resid.shape
+    capacity = prev_rows.shape[3]
+    units = down.shape[1]
+    strips = units // LANES
+    depth = n // 4
+    tokens = n * rows
+    smem = pl.BlockSpec(memory_space=pltpu.SMEM)
+    vmem = pl.BlockSpec(memory_space=pltpu.VMEM)
+    anywhere = pl.BlockSpec(memory_space=pl.ANY)
+    block = (rows, features)
+    dma = pltpu.SemaphoreType.DMA
+    attended_shape = query.shape[:2] + (LATENT,)
+    return pl.pallas_call(
+        functools.partial(fused_kernel, n),
+        out_shape=(
+            jax.ShapeDtypeStruct(attended_shape, BF16),
+            jax.ShapeDtypeStruct(block, BF16),
+        ),
+        in_specs=[smem, smem] + [vmem] * 6 + [anywhere] * 5,
+        out_specs=(anywhere, vmem),
+        scratch_shapes=[
+            pltpu.VMEM((n, capacity, features), BF16),
+            pltpu.VMEM((n * capacity, features), F32),
+            pltpu.VMEM(query.shape, BF16),
+            pltpu.VMEM(cache.shape, BF16),
+            pltpu.VMEM(attended_shape, BF16),
+            pltpu.VMEM((strips, features, 2, LANES), BF16),
+            pltpu.VMEM((units, features), BF16),
+            pltpu.VMEM((n, rows, features + 2 * LANES), BF16),
+            pltpu.VMEM((2 * tokens, 2 * features), BF16),
+            pltpu.VMEM((strips // 2, tokens, 2 * LANES), BF16),
+            pltpu.VMEM((n,) + block, F32),
+            pltpu.VMEM((n,) + block, BF16),
+            pltpu.VMEM((2 * depth,) + block, BF16),
+            pltpu.VMEM((depth,) + block, BF16),
+            pltpu.VMEM((depth,) + block, BF16),
+            pltpu.VMEM((depth,) + block, BF16),
+            pltpu.VMEM((depth,) + block, BF16),
+            pltpu.VMEM(block, F32),
+            dma((5,)),
+            dma((strips,)),
+            dma((n,)),
+            dma((n,)),
+            dma((n,)),
+            dma((n,)),
+            dma((n,)),
+            dma((n,)),
+        ],
+        compiler_params=pltpu.CompilerParams(
+            collective_id=0, has_side_effects=True, vmem_limit_bytes=56 * 2**20
+        ),
+        name="fused_step",
+    )(
+        lengths,
+        slot_expert,
+        resid,
+        prev_slots.T,
+        prev_gates.T,
+        norm_gain.reshape(1, features),
+        router.T,
+        expert_ids.T,
+        prev_rows,
+        query,
+        cache,
+        gate_up,
+        down,
+    )
+
+
 def solution(mesh):
+    fused = mesh.shape["local"] == 1 and mesh.shape["node"] % 4 == 0
     return jax.shard_map(
-        shards,
+        fused_shards if fused else shards,
         mesh=mesh,
         in_specs=(
             P(("groups", "node", "local"), None),

time: 85.5 us -> 58.8 us (0.69)
  Pallas kernels: 0 us -> 53.2 us
  waiting for transfers between devices: 19.5 us -> 0 us
  matrix products: 18.6 us -> 0 us
  local copies, waits for them, and re-layouts: 22.8 us -> 4.64 us
  starting transfers between devices: 17.4 us -> 0 us
  other arithmetic: 5.59 us -> 0 us
    pallas_call x0 -> x1, Pallas kernels: none -> 53.2 us  [fused_shards(): pl.pallas_call(functools.partial(fused_kernel, n), out_shape=(jax.ShapeDt...]
    all_to_all x3 -> x0, waiting for transfers between devices: 19.5 us -> none  [the longest x1 10.3 us: shards(): lax.all_to_all(prev_rows.reshape(slot_count, capacity, features), 'node',...]
    dot_general x8 -> x0, matrix products: 18.6 us -> none  [the longest x1 7.82 us: expert_partial(): jnp.dot(flat_rows, gate_up.reshape(features, 2 * unit_count), preferred_e...]
    all_to_all x3 -> x0, starting transfers between devices: 17.4 us -> none  [the longest x1 7.53 us: shards(): lax.all_to_all(prev_rows.reshape(slot_count, capacity, features), 'node',...]
    unnamed x25 -> x2, local copies, waits for them, and re-layouts: 19.2 us -> 3.31 us
    reduce_sum x5 -> x0, other arithmetic: 2.25 us -> none  [the longest x1 1.01 us: shards(): mean_square = jnp.mean(residual * residual, axis=1, keepdims=True)]
    convert_element_type x3 -> x0, other arithmetic: 1.64 us -> none  [the longest x1 0.92 us: shards(): (residual * lax.rsqrt(mean_square + 1e-06) * norm_gain[None, :]).astype(j...]
    convert_element_type x1 -> x0, local copies, waits for them, and re-layouts: 1.13 us -> none  [shards(): summed.astype(jnp.bfloat16).reshape(slot_count, capacity, features)]
  transfers between devices with their start and end apart: 3 -> 0, of which waited for: 2 -> 0; matrix products, arithmetic and copies ran while one was open for 30% -> 0% of each run, Pallas kernels for 0% -> 0%
where the time goes in v1:
time: 58.8 us; the launch traced here: 58.5 us
  Pallas kernels  53.2 us (90%)
  local copies, waits for them, and re-layouts  4.64 us (8%)
  between operations  0.64 us (1%)
    pallas_call x1, Pallas kernels, fused_shards(): pl.pallas_call(functools.partial(fused_kernel, n), out_shape=(jax.ShapeDt...  53.2 us
    unnamed x2, local copies, waits for them, and re-layouts  3.31 us
    reshape x1, local copies, waits for them, and re-layouts, fused_shards(): norm_gain.reshape(1, features)  1.33 us

profile of v1, /device:TPU:0, one launch (start us, length us, event | category | flops | bytes accessed | tf_op | source)
XLA Modules:
  0.0 58.5 jit_solution(8842477109250056429)
XLA Ops:
  0.6 1.3 %reshape.7.gain_ref = f32[1,3584]{1,0:T(1,128)} reshape(f32[3584]{0:T(1024)} %param.20) | data formatting | bytes 28672 | tf_op jit(solution)/shard_map/reshape | solution.py:554
  2.0 53.2 %fused_step.1 = (bf16[8,64,512]{2,1,0:T(8,128)(2,1)}, bf16[8,3584]{1,0:T(8,128)(2,1)}) custom-call(s32[8]{0:T(128)} %lengths_ref.1, s32[16]{0:T(128)} %slot_expert_ref.1, bf16[8,3584]{1,0:T(8,128)(2,1)} %resid_ref.1, s32[4,8]{1,0:T(4,128)} %bitcast.5, f32[4,8]{1,0:T(4,128)} %bitcast.6, f32[1,3584]{1,0:T(1,128)} %reshape.7.gain_ref, ...), custom_call_target="tpu_custom_call" | custom-call | tf_op jit(solution)/shard_map/fused_step/pallas_call | solution.py:508
  55.2 1.9 %copy.17 = bf16[8,64,512]{2,1,0:T(8,128)(2,1)} copy(bf16[8,64,512]{2,1,0:T(8,128)(2,1)} %get-tuple-element.4) | data formatting | bytes 1048576
  57.1 1.4 %copy.18 = bf16[8,3584]{1,0:T(8,128)(2,1)} copy(bf16[8,3584]{1,0:T(8,128)(2,1)} %get-tuple-element.5) | data formatting | bytes 114688

commit v2 on v1

--- a/solution.py
+++ b/solution.py
@@ -185,7 +185,9 @@
     wide_v,
     down_v,
     blocks,
-    spread,
+    gate_v,
+    up_v,
+    tokens_v,
     hidden_v,
     partial_v,
     out_blocks,
@@ -297,13 +299,34 @@
     gate_low = (rest - gate_mid.astype(F32)).astype(BF16)
 
     slot_lane = lax.broadcasted_iota(jnp.int32, (1, LANES), 1)
+    half = LANES // 2
     held = jnp.full((1, LANES), -1, jnp.int32)
     for i in range(n):
-        held = jnp.where(slot_lane == i, slot_expert_ref[i], held)
+        held = jnp.where(slot_lane % half == i, slot_expert_ref[i], held)
     first = jnp.ones((1, LANES), F32)
     for i in range(n):
-        first = jnp.where((held == slot_expert_ref[i]) & (slot_lane > i), 0.0, first)
+        first = jnp.where((held == slot_expert_ref[i]) & (slot_lane % half > i), 0.0, first)
     held = held.astype(F32)
+
+    row = lax.broadcasted_iota(jnp.int32, (2 * LANES, 2 * LANES), 0)
+    column = lax.broadcasted_iota(jnp.int32, (2 * LANES, 2 * LANES), 1)
+    parting = jnp.where(
+        ((row < LANES) & (column == 2 * row))
+        | ((row >= LANES) & (column == 2 * (row - LANES) + 1)),
+        1.0,
+        0.0,
+    ).astype(BF16)
+    for p in range(strips // 2):
+        strip_copy(2 * p).wait()
+        strip_copy(2 * p + 1).wait()
+        left, right = (wide_v.at[2 * p + i].reshape(2 * features, LANES) for i in range(2))
+        for b in range(features // LANES):
+            span = slice(b * 2 * LANES, (b + 1) * 2 * LANES)
+            mixed = jnp.concatenate([left[span, :], right[span, :]], axis=1)
+            apart = jnp.dot(parting, mixed, preferred_element_type=F32).astype(BF16)
+            rows_of = slice(b * LANES, (b + 1) * LANES)
+            gate_v[rows_of, p * 2 * LANES : (p + 1) * 2 * LANES] = apart[:LANES]
+            up_v[rows_of, p * 2 * LANES : (p + 1) * 2 * LANES] = apart[LANES:]
 
     own_prev.wait()
 
@@ -327,7 +350,7 @@
     residual = resid_ref[...].astype(F32) + combined
     residual_v[...] = residual
     mean_square = jnp.sum(residual * residual, axis=1, keepdims=True) * (1.0 / features)
-    normed = (residual * lax.rsqrt(mean_square + 1e-06) * gain_ref[...]).astype(BF16)
+    normed = (residual * lax.rsqrt(mean_square + 1e-06) * gain_ref[...].reshape(1, features)).astype(BF16)
     logits = lax.dot_general(
         normed, router_ref[...], (((1,), (1,)), ((), ())), preferred_element_type=F32
     )
@@ -346,77 +369,85 @@
     weight_high = slot_weight.astype(BF16)
     weight_low = (slot_weight - weight_high.astype(F32)).astype(BF16)
     blocks[me, :, :features] = normed
-    blocks[me, :, features : features + LANES] = weight_high
-    blocks[me, :, features + LANES :] = weight_low
+    blocks[me, :, features:] = jnp.where(
+        lax.broadcasted_iota(jnp.int32, slot_weight.shape, 1) < half,
+        weight_high.astype(F32),
+        weight_low.astype(F32),
+    ).astype(BF16)
 
     across, sibling = z * 4 + (1 - y) * 2 + c, z * 4 + y * 2 + (1 - c)
     started = []
 
-    def send_block(index, peer):
-        copy = remote(
-            blocks.at[index], blocks.at[index], gather_send.at[len(started)],
+    def index_of(line):
+        return line * 4 + y * 2 + c
+
+    def block_copy(index, send_index, peer):
+        return remote(
+            blocks.at[index], blocks.at[index], gather_send.at[send_index],
             gather_recv.at[index], peer,
         )
+
+    def send_block(index, peer):
+        copy = block_copy(index, len(started), peer)
         copy.start()
         started.append(copy)
 
     def await_block(index):
-        remote(
-            blocks.at[index], blocks.at[index], gather_send.at[0], gather_recv.at[index], sibling
-        ).wait_recv()
-
-    for d in range(1, depth):
-        send_block(me, lax.rem(z + d, depth) * 4 + y * 2 + c)
+        block_copy(index, 0, sibling).wait_recv()
+
+    def line_copy(way, d):
+        return block_copy(index_of(z - way * d), n + (1 + way) * depth // 2 + d, index_of(z + way))
+
+    def passes_on(way, d):
+        source, target = z - way * d, z + way
+        return (source >= 0) & (source < depth) & (target >= 0) & (target < depth)
+
+    for way in (1, -1):
+        pl.when(passes_on(way, 0))(line_copy(way, 0).start)
     send_block(me, across)
     send_block(me, sibling)
-    await_block(across)
-    send_block(across, sibling)
     for d in range(1, depth):
-        other = lax.rem(z + d, depth) * 4 + y * 2 + c
-        await_block(other)
-        send_block(other, across)
-        send_block(other, sibling)
+        for way in (1, -1):
+            source = z - way * d
+
+            @pl.when((source >= 0) & (source < depth))
+            def _():
+                await_block(index_of(source))
+                pl.when(passes_on(way, d))(line_copy(way, d).start)
+                side = block_copy(index_of(source), 2 + source, across)
+                side.start()
+                near = block_copy(index_of(source), 2 + depth + source, sibling)
+                near.start()
+        if d == 1:
+            await_block(across)
+            block_copy(across, 2 + 2 * depth, sibling).start()
     for d in range(1, depth):
-        other = lax.rem(z + d, depth) * 4 + (1 - y) * 2 + c
-        await_block(other)
-        send_block(other, sibling)
+        for way in (1, -1):
+            source = z - way * d
+
+            @pl.when((source >= 0) & (source < depth))
+            def _():
+                other = source * 4 + (1 - y) * 2 + c
+                await_block(other)
+                block_copy(other, 3 + 2 * depth + source, sibling).start()
     for d in range(depth):
         for side in range(2):
             await_block(lax.rem(z + d, depth) * 4 + side * 2 + (1 - c))
-    for i in range(strips):
-        strip_copy(i).wait()
 
     tokens = n * rows
-    low = lax.broadcasted_iota(jnp.int32, (LANES, 4 * LANES), 0)
-    high = lax.broadcasted_iota(jnp.int32, (LANES, 4 * LANES), 1)
-    dealt = jnp.where(
-        (high == 2 * low) | (high == 2 * low + 1 + 2 * LANES), 1.0, 0.0
-    ).astype(BF16)
     for b in range(features // LANES):
-        part = blocks[:, :, b * LANES : (b + 1) * LANES].astype(F32).reshape(tokens, LANES)
-        both = jnp.dot(part.astype(BF16), dealt, preferred_element_type=F32).astype(BF16)
-        spread[:tokens, b * 2 * LANES : (b + 1) * 2 * LANES] = both[:, : 2 * LANES]
-        spread[tokens:, b * 2 * LANES : (b + 1) * 2 * LANES] = both[:, 2 * LANES :]
-    tail = blocks[:, :, features:].astype(F32).reshape(tokens, 2 * LANES)
+        span = slice(b * LANES, (b + 1) * LANES)
+        tokens_v[:, span] = blocks[:, :, span].astype(F32).reshape(tokens, LANES).astype(BF16)
+    tail = blocks[:, :, features:].astype(F32).reshape(tokens, LANES)
     tail_lane = lax.broadcasted_iota(jnp.int32, tail.shape, 1)
     mine = jnp.sum(
-        jnp.where((tail_lane == me) | (tail_lane == me + LANES), tail, 0.0), axis=1, keepdims=True
-    )
-
-    def project(p, carry):
-        weights = jnp.concatenate(
-            [
-                wide_v.at[2 * p].reshape(2 * features, LANES)[...],
-                wide_v.at[2 * p + 1].reshape(2 * features, LANES)[...],
-            ],
-            axis=1,
-        )
-        projected = jnp.dot(spread[...], weights, preferred_element_type=F32)
-        gate, up = projected[:tokens], projected[tokens:]
+        jnp.where((tail_lane == me) | (tail_lane == me + half), tail, 0.0), axis=1, keepdims=True
+    )
+    for p in range(strips // 2):
+        span = slice(p * 2 * LANES, (p + 1) * 2 * LANES)
+        gate = jnp.dot(tokens_v[...], gate_v[:, span], preferred_element_type=F32)
+        up = jnp.dot(tokens_v[...], up_v[:, span], preferred_element_type=F32)
         hidden_v[p] = (gate / (1.0 + jnp.exp(-gate)) * up).astype(BF16)
-        return carry
-
-    lax.fori_loop(0, strips // 2, project, 0)
     down_copy.wait()
     hidden = jnp.concatenate([hidden_v[p] for p in range(strips // 2)], axis=1)
     step = 512
@@ -437,8 +468,9 @@
     def await_sum(dst, index):
         remote(dst, dst, sum_send.at[0], sum_recv.at[index], sibling).wait_recv()
 
-    order = list(range(1, depth)) + [0]
-    lines = [lax.rem(z + d, depth) for d in order]
+    lines = []
+    for d in range(depth // 2):
+        lines += [depth - 1 - d, d]
     for line in lines:
         for side in (1 - y, y):
             send_sum(
@@ -452,20 +484,56 @@
         send_sum(side_out.at[line], side_in.at[line], len(sums), 2 * depth + line, across)
         await_sum(core_in.at[line * 2 + y], line * 2 + y)
         partial_v[line * 4 + y * 2 + c] += core_in[line * 2 + y].astype(F32)
+
+    def far_copy(way, line):
+        return remote(
+            far_out.at[line], far_in.at[(1 + way) // 2, line], sum_send.at[3 * depth + line],
+            sum_recv.at[(4 - way) * depth + line], index_of(z + way),
+        )
+
+    def take_far(way, line):
+        far_copy(way, line).wait_recv()
+        partial_v[index_of(line)] += far_in[(1 + way) // 2, line].astype(F32)
+
     for line in lines:
         await_sum(side_in.at[line], 2 * depth + line)
-        value = partial_v[line * 4 + y * 2 + c] + side_in[line].astype(F32)
-        if line is lines[-1]:
-            residual_v[...] += value
-        else:
-            far_out[line] = value.astype(BF16)
-            send_sum(
-                far_out.at[line], far_in.at[z], len(sums), 3 * depth + z, line * 4 + y * 2 + c
-            )
-    for line in lines[:-1]:
-        await_sum(far_in.at[line], 3 * depth + line)
-        residual_v[...] += far_in[line].astype(F32)
-    mixed_ref[...] = residual_v[...].astype(BF16)
+        partial_v[index_of(line)] += side_in[line].astype(F32)
+
+        @pl.when(z < line)
+        def _():
+            pl.when(z > 0)(lambda: take_far(1, line))
+            far_out[line] = partial_v[index_of(line)].astype(BF16)
+            far_copy(1, line).start()
+
+        @pl.when(z > line)
+        def _():
+            pl.when(z < depth - 1)(lambda: take_far(-1, line))
+            far_out[line] = partial_v[index_of(line)].astype(BF16)
+            far_copy(-1, line).start()
+
+    for line in range(depth):
+        @pl.when(z == line)
+        def _():
+            if line > 0:
+                take_far(1, line)
+            if line < depth - 1:
+                take_far(-1, line)
+
+    mixed_ref[...] = residual_v[...] + partial_v[me]
+
+    for line in range(depth):
+        pl.when(z < line)(lambda: far_copy(1, line).wait_send())
+        pl.when(z > line)(lambda: far_copy(-1, line).wait_send())
+    for d in range(depth):
+        for way in (1, -1):
+            pl.when(passes_on(way, d))(lambda: line_copy(way, d).wait_send())
+    block_copy(across, 2 + 2 * depth, sibling).wait_send()
+    for d in range(1, depth):
+        source = lax.rem(z + d, depth)
+        other = source * 4 + (1 - y) * 2 + c
+        block_copy(index_of(source), 2 + source, across).wait_send()
+        block_copy(index_of(source), 2 + depth + source, sibling).wait_send()
+        block_copy(other, 3 + 2 * depth + source, sibling).wait_send()
 
     def sent_prev(step, carry):
         prev_copy(step).wait_send()
@@ -505,11 +573,11 @@
     block = (rows, features)
     dma = pltpu.SemaphoreType.DMA
     attended_shape = query.shape[:2] + (LATENT,)
-    return pl.pallas_call(
+    attended, mixed = pl.pallas_call(
         functools.partial(fused_kernel, n),
         out_shape=(
             jax.ShapeDtypeStruct(attended_shape, BF16),
-            jax.ShapeDtypeStruct(block, BF16),
+            jax.ShapeDtypeStruct(block, F32),
         ),
         in_specs=[smem, smem] + [vmem] * 6 + [anywhere] * 5,
         out_specs=(anywhere, vmem),
@@ -521,8 +589,10 @@
             pltpu.VMEM(attended_shape, BF16),
             pltpu.VMEM((strips, features, 2, LANES), BF16),
             pltpu.VMEM((units, features), BF16),
-            pltpu.VMEM((n, rows, features + 2 * LANES), BF16),
-            pltpu.VMEM((2 * tokens, 2 * features), BF16),
+            pltpu.VMEM((n, rows, features + LANES), BF16),
+            pltpu.VMEM((features, units), BF16),
+            pltpu.VMEM((features, units), BF16),
+            pltpu.VMEM((tokens, features), BF16),
             pltpu.VMEM((strips // 2, tokens, 2 * LANES), BF16),
             pltpu.VMEM((n,) + block, F32),
             pltpu.VMEM((n,) + block, BF16),
@@ -530,19 +600,19 @@
             pltpu.VMEM((depth,) + block, BF16),
             pltpu.VMEM((depth,) + block, BF16),
             pltpu.VMEM((depth,) + block, BF16),
-            pltpu.VMEM((depth,) + block, BF16),
+            pltpu.VMEM((2, depth) + block, BF16),
             pltpu.VMEM(block, F32),
             dma((5,)),
             dma((strips,)),
             dma((n,)),
             dma((n,)),
+            dma((2 * n,)),
             dma((n,)),
             dma((n,)),
-            dma((n,)),
-            dma((n,)),
+            dma((2 * n,)),
         ],
         compiler_params=pltpu.CompilerParams(
-            collective_id=0, has_side_effects=True, vmem_limit_bytes=56 * 2**20
+            collective_id=0, has_side_effects=True, vmem_limit_bytes=58 * 2**20
         ),
         name="fused_step",
     )(
@@ -551,7 +621,7 @@
         resid,
         prev_slots.T,
         prev_gates.T,
-        norm_gain.reshape(1, features),
+        norm_gain,
         router.T,
         expert_ids.T,
         prev_rows,
@@ -560,6 +630,7 @@
         gate_up,
         down,
     )
+    return attended, mixed.astype(BF16)
 
 
 def solution(mesh):

time: 58.8 us -> 63.1 us (1.073)
  Pallas kernels: 53.2 us -> 58.8 us
  local copies, waits for them, and re-layouts: 4.64 us -> 1.87 us
  other arithmetic: 0 us -> 1.53 us
    pallas_call x1, Pallas kernels: 53.2 us -> 58.8 us  [fused_shards(): pl.pallas_call(functools.partial(fused_kernel, n), out_shape=(jax.ShapeDt...]
    convert_element_type x0 -> x1, other arithmetic: none -> 1.53 us  [fused_shards(): return (attended, mixed.astype(BF16))]
    unnamed x2 -> x1, local copies, waits for them, and re-layouts: 3.31 us -> 1.87 us
    reshape x1 -> x0, local copies, waits for them, and re-layouts: 1.33 us -> none  [fused_shards(): norm_gain.reshape(1, features)]
where the time goes in v2:
time: 63.1 us; the launch traced here: 62.9 us
  Pallas kernels  58.8 us (93%)
  local copies, waits for them, and re-layouts  1.87 us (3%)
  other arithmetic  1.53 us (2%)
  between operations  0.64 us (1%)
    pallas_call x1, Pallas kernels, fused_shards(): pl.pallas_call(functools.partial(fused_kernel, n), out_shape=(jax.ShapeDt...  58.8 us
    unnamed x1, local copies, waits for them, and re-layouts  1.87 us
    convert_element_type x1, other arithmetic, fused_shards(): return (attended, mixed.astype(BF16))  1.53 us

profile of v2, /device:TPU:0, one launch (start us, length us, event | category | flops | bytes accessed | tf_op | source)
XLA Modules:
  0.0 62.9 jit_solution(1321174550034084195)
XLA Ops:
  0.6 58.8 %fused_step.1 = (bf16[8,64,512]{2,1,0:T(8,128)(2,1)}, f32[8,3584]{1,0:T(8,128)}) custom-call(s32[8]{0:T(128)} %lengths_ref.1, s32[16]{0:T(128)} %slot_expert_ref.1, bf16[8,3584]{1,0:T(8,128)(2,1)} %resid_ref.1, s32[4,8]{1,0:T(4,128)} %bitcast.5, f32[4,8]{1,0:T(4,128)} %bitcast.6, f32[3584]{0:T(1024)} %gain_ref.1, bf16[14,3584]{1,0:T(8,128)(2,1)} %bitcast.4, ...), custom_call_target="tpu_custom_call" | custom-call | tf_op jit(solution)/shard_map/fused_step/pallas_call | solution.py:576
  59.5 1.5 %convert_element_type.3 = bf16[8,3584]{1,0:T(8,128)(2,1)} convert(f32[8,3584]{1,0:T(8,128)} %get-tuple-element.5) | non-fusion elementwise | flops 28672 | bytes 172032 | tf_op jit(solution)/shard_map/convert_element_type | solution.py:633
  61.0 1.9 %copy.16 = bf16[8,64,512]{2,1,0:T(8,128)(2,1)} copy(bf16[8,64,512]{2,1,0:T(8,128)(2,1)} %get-tuple-element.8) | data formatting | bytes 1048576

commit v3 on v1

--- a/solution.py
+++ b/solution.py
@@ -185,7 +185,9 @@
     wide_v,
     down_v,
     blocks,
-    spread,
+    gate_v,
+    up_v,
+    tokens_v,
     hidden_v,
     partial_v,
     out_blocks,
@@ -297,14 +299,38 @@
     gate_low = (rest - gate_mid.astype(F32)).astype(BF16)
 
     slot_lane = lax.broadcasted_iota(jnp.int32, (1, LANES), 1)
+    half = LANES // 2
     held = jnp.full((1, LANES), -1, jnp.int32)
     for i in range(n):
-        held = jnp.where(slot_lane == i, slot_expert_ref[i], held)
+        held = jnp.where(slot_lane % half == i, slot_expert_ref[i], held)
     first = jnp.ones((1, LANES), F32)
     for i in range(n):
-        first = jnp.where((held == slot_expert_ref[i]) & (slot_lane > i), 0.0, first)
+        first = jnp.where((held == slot_expert_ref[i]) & (slot_lane % half > i), 0.0, first)
     held = held.astype(F32)
 
+    row = lax.broadcasted_iota(jnp.int32, (2 * LANES, 2 * LANES), 0)
+    column = lax.broadcasted_iota(jnp.int32, (2 * LANES, 2 * LANES), 1)
+    parting = jnp.where(
+        ((row < LANES) & (column == 2 * row))
+        | ((row >= LANES) & (column == 2 * (row - LANES) + 1)),
+        1.0,
+        0.0,
+    ).astype(BF16)
+
+    def part(p):
+        strip_copy(2 * p).wait()
+        strip_copy(2 * p + 1).wait()
+        left, right = (wide_v.at[2 * p + i].reshape(2 * features, LANES) for i in range(2))
+        for b in range(features // LANES):
+            span = slice(b * 2 * LANES, (b + 1) * 2 * LANES)
+            mixed = jnp.concatenate([left[span, :], right[span, :]], axis=1)
+            apart = jnp.dot(parting, mixed, preferred_element_type=F32).astype(BF16)
+            rows_of = slice(b * LANES, (b + 1) * LANES)
+            gate_v[rows_of, p * 2 * LANES : (p + 1) * 2 * LANES] = apart[:LANES]
+            up_v[rows_of, p * 2 * LANES : (p + 1) * 2 * LANES] = apart[LANES:]
+
+    for p in range(strips // 2 - 1):
+        part(p)
     own_prev.wait()
 
     def take_prev(step, carry):
@@ -327,7 +353,7 @@
     residual = resid_ref[...].astype(F32) + combined
     residual_v[...] = residual
     mean_square = jnp.sum(residual * residual, axis=1, keepdims=True) * (1.0 / features)
-    normed = (residual * lax.rsqrt(mean_square + 1e-06) * gain_ref[...]).astype(BF16)
+    normed = (residual * lax.rsqrt(mean_square + 1e-06) * gain_ref[...].reshape(1, features)).astype(BF16)
     logits = lax.dot_general(
         normed, router_ref[...], (((1,), (1,)), ((), ())), preferred_element_type=F32
     )
@@ -346,8 +372,11 @@
     weight_high = slot_weight.astype(BF16)
     weight_low = (slot_weight - weight_high.astype(F32)).astype(BF16)
     blocks[me, :, :features] = normed
-    blocks[me, :, features : features + LANES] = weight_high
-    blocks[me, :, features + LANES :] = weight_low
+    blocks[me, :, features:] = jnp.where(
+        lax.broadcasted_iota(jnp.int32, slot_weight.shape, 1) < half,
+        weight_high.astype(F32),
+        weight_low.astype(F32),
+    ).astype(BF16)
 
     across, sibling = z * 4 + (1 - y) * 2 + c, z * 4 + y * 2 + (1 - c)
     started = []
@@ -369,6 +398,7 @@
         send_block(me, lax.rem(z + d, depth) * 4 + y * 2 + c)
     send_block(me, across)
     send_block(me, sibling)
+    part(strips // 2 - 1)
     await_block(across)
     send_block(across, sibling)
     for d in range(1, depth):
@@ -383,40 +413,20 @@
     for d in range(depth):
         for side in range(2):
             await_block(lax.rem(z + d, depth) * 4 + side * 2 + (1 - c))
-    for i in range(strips):
-        strip_copy(i).wait()
-
     tokens = n * rows
-    low = lax.broadcasted_iota(jnp.int32, (LANES, 4 * LANES), 0)
-    high = lax.broadcasted_iota(jnp.int32, (LANES, 4 * LANES), 1)
-    dealt = jnp.where(
-        (high == 2 * low) | (high == 2 * low + 1 + 2 * LANES), 1.0, 0.0
-    ).astype(BF16)
     for b in range(features // LANES):
-        part = blocks[:, :, b * LANES : (b + 1) * LANES].astype(F32).reshape(tokens, LANES)
-        both = jnp.dot(part.astype(BF16), dealt, preferred_element_type=F32).astype(BF16)
-        spread[:tokens, b * 2 * LANES : (b + 1) * 2 * LANES] = both[:, : 2 * LANES]
-        spread[tokens:, b * 2 * LANES : (b + 1) * 2 * LANES] = both[:, 2 * LANES :]
-    tail = blocks[:, :, features:].astype(F32).reshape(tokens, 2 * LANES)
+        span = slice(b * LANES, (b + 1) * LANES)
+        tokens_v[:, span] = blocks[:, :, span].astype(F32).reshape(tokens, LANES).astype(BF16)
+    tail = blocks[:, :, features:].astype(F32).reshape(tokens, LANES)
     tail_lane = lax.broadcasted_iota(jnp.int32, tail.shape, 1)
     mine = jnp.sum(
-        jnp.where((tail_lane == me) | (tail_lane == me + LANES), tail, 0.0), axis=1, keepdims=True
-    )
-
-    def project(p, carry):
-        weights = jnp.concatenate(
-            [
-                wide_v.at[2 * p].reshape(2 * features, LANES)[...],
-                wide_v.at[2 * p + 1].reshape(2 * features, LANES)[...],
-            ],
-            axis=1,
-        )
-        projected = jnp.dot(spread[...], weights, preferred_element_type=F32)
-        gate, up = projected[:tokens], projected[tokens:]
+        jnp.where((tail_lane == me) | (tail_lane == me + half), tail, 0.0), axis=1, keepdims=True
+    )
+    for p in range(strips // 2):
+        span = slice(p * 2 * LANES, (p + 1) * 2 * LANES)
+        gate = jnp.dot(tokens_v[...], gate_v[:, span], preferred_element_type=F32)
+        up = jnp.dot(tokens_v[...], up_v[:, span], preferred_element_type=F32)
         hidden_v[p] = (gate / (1.0 + jnp.exp(-gate)) * up).astype(BF16)
-        return carry
-
-    lax.fori_loop(0, strips // 2, project, 0)
     down_copy.wait()
     hidden = jnp.concatenate([hidden_v[p] for p in range(strips // 2)], axis=1)
     step = 512
@@ -465,7 +475,7 @@
     for line in lines[:-1]:
         await_sum(far_in.at[line], 3 * depth + line)
         residual_v[...] += far_in[line].astype(F32)
-    mixed_ref[...] = residual_v[...].astype(BF16)
+    mixed_ref[...] = residual_v[...]
 
     def sent_prev(step, carry):
         prev_copy(step).wait_send()
@@ -505,11 +515,11 @@
     block = (rows, features)
     dma = pltpu.SemaphoreType.DMA
     attended_shape = query.shape[:2] + (LATENT,)
-    return pl.pallas_call(
+    attended, mixed = pl.pallas_call(
         functools.partial(fused_kernel, n),
         out_shape=(
             jax.ShapeDtypeStruct(attended_shape, BF16),
-            jax.ShapeDtypeStruct(block, BF16),
+            jax.ShapeDtypeStruct(block, F32),
         ),
         in_specs=[smem, smem] + [vmem] * 6 + [anywhere] * 5,
         out_specs=(anywhere, vmem),
@@ -521,8 +531,10 @@
             pltpu.VMEM(attended_shape, BF16),
             pltpu.VMEM((strips, features, 2, LANES), BF16),
             pltpu.VMEM((units, features), BF16),
-            pltpu.VMEM((n, rows, features + 2 * LANES), BF16),
-            pltpu.VMEM((2 * tokens, 2 * features), BF16),
+            pltpu.VMEM((n, rows, features + LANES), BF16),
+            pltpu.VMEM((features, units), BF16),
+            pltpu.VMEM((features, units), BF16),
+            pltpu.VMEM((tokens, features), BF16),
             pltpu.VMEM((strips // 2, tokens, 2 * LANES), BF16),
             pltpu.VMEM((n,) + block, F32),
             pltpu.VMEM((n,) + block, BF16),
@@ -542,7 +554,7 @@
             dma((n,)),
         ],
         compiler_params=pltpu.CompilerParams(
-            collective_id=0, has_side_effects=True, vmem_limit_bytes=56 * 2**20
+            collective_id=0, has_side_effects=True, vmem_limit_bytes=58 * 2**20
         ),
         name="fused_step",
     )(
@@ -551,7 +563,7 @@
         resid,
         prev_slots.T,
         prev_gates.T,
-        norm_gain.reshape(1, features),
+        norm_gain,
         router.T,
         expert_ids.T,
         prev_rows,
@@ -560,6 +572,7 @@
         gate_up,
         down,
     )
+    return attended, mixed.astype(BF16)
 
 
 def solution(mesh):

time: 58.8 us -> 51.8 us (0.88)
  Pallas kernels: 53.2 us -> 47.5 us
  local copies, waits for them, and re-layouts: 4.64 us -> 1.87 us
  other arithmetic: 0 us -> 1.53 us
    pallas_call x1, Pallas kernels: 53.2 us -> 47.5 us  [fused_shards(): pl.pallas_call(functools.partial(fused_kernel, n), out_shape=(jax.ShapeDt...]
    convert_element_type x0 -> x1, other arithmetic: none -> 1.53 us  [fused_shards(): return (attended, mixed.astype(BF16))]
    unnamed x2 -> x1, local copies, waits for them, and re-layouts: 3.31 us -> 1.87 us
    reshape x1 -> x0, local copies, waits for them, and re-layouts: 1.33 us -> none  [fused_shards(): norm_gain.reshape(1, features)]
where the time goes in v3:
time: 51.8 us; the launch traced here: 51.6 us
  Pallas kernels  47.5 us (92%)
  local copies, waits for them, and re-layouts  1.87 us (4%)
  other arithmetic  1.53 us (3%)
  between operations  0.64 us (1%)
    pallas_call x1, Pallas kernels, fused_shards(): pl.pallas_call(functools.partial(fused_kernel, n), out_shape=(jax.ShapeDt...  47.5 us
    unnamed x1, local copies, waits for them, and re-layouts  1.87 us
    convert_element_type x1, other arithmetic, fused_shards(): return (attended, mixed.astype(BF16))  1.53 us

profile of v3, /device:TPU:0, one launch (start us, length us, event | category | flops | bytes accessed | tf_op | source)
XLA Modules:
  0.0 51.6 jit_solution(17403206706479069361)
XLA Ops:
  0.6 47.5 %fused_step.1 = (bf16[8,64,512]{2,1,0:T(8,128)(2,1)}, f32[8,3584]{1,0:T(8,128)}) custom-call(s32[8]{0:T(128)} %lengths_ref.1, s32[16]{0:T(128)} %slot_expert_ref.1, bf16[8,3584]{1,0:T(8,128)(2,1)} %resid_ref.1, s32[4,8]{1,0:T(4,128)} %bitcast.5, f32[4,8]{1,0:T(4,128)} %bitcast.6, f32[3584]{0:T(1024)} %gain_ref.1, bf16[14,3584]{1,0:T(8,128)(2,1)} %bitcast.4, ...), custom_call_target="tpu_custom_call" | custom-call | tf_op jit(solution)/shard_map/fused_step/pallas_call | solution.py:518
  48.2 1.5 %convert_element_type.3 = bf16[8,3584]{1,0:T(8,128)(2,1)} convert(f32[8,3584]{1,0:T(8,128)} %get-tuple-element.5) | non-fusion elementwise | flops 28672 | bytes 172032 | tf_op jit(solution)/shard_map/convert_element_type | solution.py:575
  49.7 1.9 %copy.16 = bf16[8,64,512]{2,1,0:T(8,128)(2,1)} copy(bf16[8,64,512]{2,1,0:T(8,128)(2,1)} %get-tuple-element.8) | data formatting | bytes 1048576
